TPU v7x, 512 devices: a whole 4x8x8 slice. The times are simulated.
512 devices in a mesh: replica: 32 (over y, x), shard: 16 (over z, core).
Axes of the slice: x: 4, y: 8, z: 8, core: 2. Of those that a mesh axis runs over, the one named last changes fastest.
Arguments:
- grads: bfloat16 [32, 256, 8192], P('replica', 'shard'), may hold values from -6 to 6
- error: float32 [32, 256, 8192], P('replica', 'shard'), may hold values from -4 to 4
- momentum: float32 [256, 8192], P('shard'), may hold values from -1 to 1
- weight: bfloat16 [256, 8192], P('shard'), may hold values from -6 to 6
- q_start: float32 [8192, 32], replicated, may hold values from -6 to 6
Outputs:
- new_error: float32 [32, 256, 8192], P('replica', 'shard')
- new_momentum: float32 [256, 8192], P('shard')
- new_weight: bfloat16 [256, 8192], P('shard')
- q_next: float32 [8192, 32], replicated
All inputs are finite; a program needn't handle non-finite values.
Results may differ from a plain program's by a relative error of at most 0.001.
Values sent between devices are 32-bit elements; how exact they have to be, the bound alone decides.
A program may use at most 64 MiB of HBM per device.

v0:
```python
import jax
import jax.numpy as jnp
from jax import lax
from jax.sharding import PartitionSpec as P


def on_device(grads, error, momentum, weight, q_start):
    highest = lax.Precision.HIGHEST
    merged = grads[0].astype(jnp.float32) + error[0]
    p_local = jnp.dot(merged, q_start, precision=highest)
    p_sum = lax.psum(p_local, "replica")
    gram = lax.psum(jnp.dot(p_sum.T, p_sum, precision=highest), "shard")
    factor = jnp.linalg.cholesky(gram)
    p_ortho = jax.scipy.linalg.solve_triangular(factor, p_sum.T, lower=True).T
    q_term = lax.dot_general(merged, p_ortho, (((0,), (0,)), ((), ())), precision=highest)
    q_total = lax.psum(q_term, ("replica", "shard"))
    q_next = q_total / lax.axis_size("replica")
    approx = jnp.dot(p_ortho, q_next.T, precision=highest)
    new_error = (merged - approx)[None]
    new_momentum = 0.9 * momentum + approx
    new_weight = (weight.astype(jnp.float32) - 0.5 * new_momentum).astype(jnp.bfloat16)
    return (new_error, new_momentum, new_weight, q_next)


def solution(mesh):
    placed = (
        P("replica", "shard", None),
        P("replica", "shard", None),
        P("shard", None),
        P("shard", None),
        P(),
    )
    return jax.shard_map(
        on_device,
        mesh=mesh,
        in_specs=placed,
        out_specs=(P("replica", "shard", None), P("shard", None), P("shard", None), P()),
        check_vma=False,
    )
```

profile of v0, /device:TPU:1, one launch (start us, length us, event | category | flops | bytes accessed | tf_op | source)
XLA Modules:
  0.0 424.6 jit_solution(4418686574348404974)
XLA Ops:
  7.2 0.0 copy-start
  7.2 0.0 all-reduce.2.cloned.1.call-start
  7.2 1.2 copy-done
  8.4 0.0 copy-start.1
  8.4 2.1 fusion.2
  10.5 0.0 copy-start.3
  10.5 63.7 %psum.21 = f32[16,32]{1,0:T(8,128)S(1)} all-reduce(f32[16,32]{1,0:T(8,128)S(1)} %fusion.2), channel_id=1, replica_groups=mesh['replica'=32,'shard'=16] {'replica'}, use_global_device_ids=true, to_apply=%region_0.0 | all-reduce | flops 512 | bytes 4096 | tf_op jit(solution)/shard_map/psum | solution.py:11
  74.2 0.2 fusion.9
  74.4 62.5 %psum.22 = f32[32,32]{0,1:T(8,128)S(1)} all-reduce(f32[32,32]{0,1:T(8,128)S(1)} %fusion.9), channel_id=1, replica_groups=mesh['replica'=32,'shard'=16] {'shard'}, use_global_device_ids=true, to_apply=%region_1.0 | all-reduce | flops 1024 | bytes 8192 | tf_op jit(solution)/shard_map/psum | solution.py:12
  136.9 0.1 copy.10
  137.0 2.9 cholesky.16
  140.0 0.6 compare_reduce_fusion
  140.6 0.7 fusion.5
  141.3 2.4 custom-call.7
  143.7 0.2 fusion.6
  143.9 0.0 copy-done.1
  143.9 0.0 copy-done.3
  143.9 2.0 fusion
  145.9 0.0 all-reduce.2.cloned.1.call-update
  145.9 0.0 copy-start.4
  145.9 0.0 copy-start.5
  145.9 268.7 %all-reduce.2.cloned.1.call-done = f32[8192,32]{0,1:T(8,128)} async-done(((f32[8192,32]{0,1:T(8,128)}), f32[8192,32]{0,1:T(8,128)}) %all-reduce.2.cloned.1.call-update) | async-done | bytes 1048592 | tf_op jit(solution)/shard_map/psum | solution.py:16
  414.6 1.3 broadcast_multiply_fusion
  415.9 0.0 copy-done.4
  415.9 0.0 copy-done.5
  416.0 0.0 copy-start.2
  416.0 1.8 subtract_convert_fusion
  417.8 0.0 copy-done.2
  (2 shorter events, 0.0 us)
Async XLA Ops:
  7.2 1.2 copy-start
  7.2 407.5 %all-reduce.2.cloned.1.call-start = ((), (), s32[]{:S(2)}) async-start(), calls=%async_computation | async-start | bytes 2097152 | tf_op jit(solution)/shard_map/psum | solution.py:16
  8.4 135.5 %copy-start.1 = (f32[1,16,8192]{2,1,0:T(8,128)S(1)}, f32[1,16,8192]{2,1,0:T(8,128)}, u32[]{:S(2)}) copy-start(f32[1,16,8192]{2,1,0:T(8,128)} %param.6) | copy-start | bytes 1572868
  10.5 133.4 %copy-start.3 = (bf16[1,16,8192]{2,1,0:T(8,128)(2,1)S(1)}, bf16[1,16,8192]{2,1,0:T(8,128)(2,1)}, u32[]{:S(2)}) copy-start(bf16[1,16,8192]{2,1,0:T(8,128)(2,1)} %param.5) | copy-start | bytes 786436
  145.9 270.0 %copy-start.4 = (f32[16,8192]{1,0:T(8,128)S(1)}, f32[16,8192]{1,0:T(8,128)}, u32[]{:S(2)}) copy-start(f32[16,8192]{1,0:T(8,128)} %param.7) | copy-start | bytes 1572868
  145.9 270.0 %copy-start.5 = (bf16[16,8192]{1,0:T(8,128)(2,1)S(1)}, bf16[16,8192]{1,0:T(8,128)(2,1)}, u32[]{:S(2)}) copy-start(bf16[16,8192]{1,0:T(8,128)(2,1)} %param.8) | copy-start | bytes 786436
  416.0 1.8 copy-start.2
Sparse Core Ops, SparseCore 0:
  146.0 268.5 all-reduce.1
where the time goes:
time: 425 us
  waiting for transfers between devices  269 us (63%)
  blocking collectives  126 us (30%)
  between operations  14.1 us (3%)
  other arithmetic  7.98 us (2%)
  matrix products  6.27 us (1%)
    psum x1, waiting for transfers between devices, on_device(): q_total = lax.psum(q_term, ('replica', 'shard'))  269 us
    psum x1, blocking collectives, on_device(): p_sum = lax.psum(p_local, 'replica')  63.7 us
    psum x1, blocking collectives, on_device(): gram = lax.psum(jnp.dot(p_sum.T, p_sum, precision=highest), 'shard')  62.5 us
  transfers between devices with their start and end apart: 1, of which 1 were waited for; matrix products, arithmetic and copies ran while one was open for 0% of the time, Pallas kernels for 0%

commit v1 on v0

v1 whole, which is shorter than its diff:
```python
import jax
import jax.numpy as jnp
from jax import lax
from jax.experimental import pallas as pl
from jax.experimental.pallas import tpu as pltpu
from jax.sharding import PartitionSpec as P

MESH = pl.DeviceIdType.MESH
HIGHEST = lax.Precision.HIGHEST
NX, NY, NZ, NC = 4, 8, 8, 2
RANK = 32
D = 8192
NT = (((1,), (1,)), ((), ()))


def send(src, dst, send_sem, recv_sem, device):
    copy = pltpu.make_async_remote_copy(
        src_ref=src, dst_ref=dst, send_sem=send_sem, recv_sem=recv_sem,
        device_id=device, device_id_type=MESH,
    )
    copy.start()
    return copy


def factor_rows(gram, pt, steps):
    sub = lax.broadcasted_iota(jnp.int32, (RANK, 1), 0)
    for j in steps:
        col = gram[:, j:j + 1]
        r = lax.rsqrt(gram[j:j + 1, j:j + 1])
        f = jnp.where(sub > j, col * r, 0.0)
        grow = gram[j:j + 1, :] * r
        prow = pt[j:j + 1, :] * r
        gram = gram - f * grow
        pt = jnp.where(sub == j, prow, pt - f * prow)
    return gram, pt


def kernel(grads, error, qs, qt, po, gbuf, ebuf, qsv, mbuf, s1buf, s1sum, s2buf, msum, mpair, mall,
           ploc, pxbuf, pxsum, pybuf, pall, oscr, load_sem, ssem, rsem):
    rep, shard = lax.axis_index("replica"), lax.axis_index("shard")
    x, y = lax.rem(rep, NX), lax.div(rep, NX)
    c, z = lax.rem(shard, NC), lax.div(shard, NC)

    def at_x(d):
        return (y * NX + lax.rem(x + d, NX), shard)

    def at_y(d):
        return (lax.rem(y + d, NY) * NX + x, shard)

    def at_z(d):
        return (rep, lax.rem(z + d, NZ) * NC + c)

    other = (rep, z * NC + (1 - c))

    slots = iter(range(64))

    def go(src, dst, device):
        k = next(slots)
        return send(src, dst, ssem.at[k], rsem.at[k], device)

    loads = []
    for g in range(NX):
        group = []
        for h in range(2):
            cols = pl.ds(h * 4096 + g * 1024, 1024)
            to = pl.ds(h * 1024, 1024)
            for i, (src, dst) in enumerate(((grads, gbuf), (error, ebuf), (qs, qsv))):
                cp = pltpu.make_async_copy(src.at[:, cols], dst.at[g, :, to], load_sem.at[g, h, i])
                cp.start()
                group.append(cp)
        loads.append(group)

    barrier = pltpu.get_barrier_semaphore()
    partners = [at_x(d) for d in range(1, NX)] + [at_y(d) for d in range(1, NY)] + [at_z(d) for d in range(1, NZ)] + [other]
    for device in partners:
        pl.semaphore_signal(barrier, inc=1, device_id=device, device_id_type=MESH)

    p = None
    for g in range(NX):
        for cp in loads[g]:
            cp.wait()
        m = gbuf[g].astype(jnp.float32) + ebuf[g]
        mbuf[g] = m
        t = lax.dot_general(m, qsv[g], NT, precision=HIGHEST, preferred_element_type=jnp.float32)
        p = t if p is None else p + t
    zero = jnp.zeros((8, 64), jnp.float32)
    packed = jnp.concatenate([p[0:8], p[8:16], zero], axis=1)
    ploc[...] = packed

    pl.semaphore_wait(barrier, len(partners))
    px = [go(ploc, pxbuf.at[x], at_x(d)) for d in range(1, NX)]
    s1 = [go(mbuf.at[lax.rem(x + d, NX)], s1buf.at[d - 1], at_x(d)) for d in range(1, NX)]

    pxbuf[x] = packed
    for cp in px:
        cp.wait_recv()
    packed = (pxbuf[0] + pxbuf[1]) + (pxbuf[2] + pxbuf[3])
    pxsum[...] = packed
    py = [go(pxsum, pybuf.at[y], at_y(d)) for d in range(1, NY)]
    pybuf[y] = packed
    for cp in py:
        cp.wait_recv()
    packed = ((pybuf[0] + pybuf[1]) + (pybuf[2] + pybuf[3])) + ((pybuf[4] + pybuf[5]) + (pybuf[6] + pybuf[7]))
    pall[z, c] = packed
    pc = go(pall.at[z, c], pall.at[z, c], other)

    for cp in s1:
        cp.wait_recv()
    for k in range(NY):
        for h in range(2):
            cols = pl.ds(h * 1024 + k * 128, 128)
            s1sum[k, h] = (mbuf[x, :, cols] + s1buf[0, :, cols]) + (s1buf[1, :, cols] + s1buf[2, :, cols])
    s2 = [go(s1sum.at[lax.rem(y + d, NY)], s2buf.at[d - 1], at_y(d)) for d in range(1, NY)]

    pc.wait_recv()
    pz = [go(pall.at[z], pall.at[z], at_z(d)) for d in range(1, NZ)]

    for cp in s2:
        cp.wait_recv()
    total = s1sum[y]
    for k in range(NY - 1):
        total = total + s2buf[k]
    msum[...] = total
    mpair[c] = msum[c]
    s3c = go(msum.at[1 - c], mpair.at[c], other)

    for cp in pz:
        cp.wait_recv()
    pt = pall[...].reshape(128, 128).T
    p0, p1 = pt[0:RANK], pt[RANK:2 * RANK]
    gram = (lax.dot_general(p0, p0, NT, precision=HIGHEST, preferred_element_type=jnp.float32)
            + lax.dot_general(p1, p1, NT, precision=HIGHEST, preferred_element_type=jnp.float32))
    pt = jnp.concatenate([p0, p1], axis=1)

    s3c.wait_recv()
    mall[z] = mpair[...]
    s3z = [go(mpair, mall.at[z], at_z(d)) for d in range(1, NZ)]
    gram, pt = factor_rows(gram, pt, range(RANK))

    for cp in s3z:
        cp.wait_recv()
    m0 = mall[:, :, 0:8, :].reshape(128, 128)
    m1 = mall[:, :, 8:16, :].reshape(128, 128)
    q = (jnp.dot(pt[:, 0:128], m0, precision=HIGHEST, preferred_element_type=jnp.float32)
         + jnp.dot(pt[:, 128:256], m1, precision=HIGHEST, preferred_element_type=jnp.float32)) * (1.0 / 32.0)

    half = c * 4096
    mine = pl.ds(pl.multiple_of(half + x * 1024 + y * 128, 128), 128)
    qt[:, mine] = q
    qy = [go(qt.at[:, mine], qt.at[:, mine], at_y(d)) for d in range(1, NY)]
    ot = jnp.concatenate([pt[:, 0:128], pt[:, 128:256]], axis=0)
    oscr[...] = jnp.concatenate([ot, jnp.zeros((64, 128), jnp.float32)], axis=0).T
    own = oscr[pl.ds(pl.multiple_of(shard * 8, 8), 8), :]
    po[0:8, :] = own[:, 0:RANK]
    po[8:16, :] = own[:, RANK:2 * RANK]
    for cp in qy:
        cp.wait_recv()
    mine = pl.ds(pl.multiple_of(half + x * 1024, 128), 1024)
    qx = [go(qt.at[:, mine], qt.at[:, mine], at_x(d)) for d in range(1, NX)]
    qc = [go(qt.at[:, mine], qt.at[:, mine], other)]
    for d in range(1, NX):
        qx[d - 1].wait_recv()
        theirs = pl.ds(pl.multiple_of(half + lax.rem(x + NX - d, NX) * 1024, 128), 1024)
        qc.append(go(qt.at[:, theirs], qt.at[:, theirs], other))
    for cp in qc:
        cp.wait_recv()
    for cp in px + s1 + py + [pc] + s2 + pz + [s3c] + s3z + qy + qx + qc:
        cp.wait_send()


def on_device(grads, error, momentum, weight, q_start):
    f32 = jnp.float32
    rows = grads.shape[1]
    vmem = pltpu.VMEM
    qt, p_ortho = pl.pallas_call(
        kernel,
        out_shape=(jax.ShapeDtypeStruct((RANK, D), f32), jax.ShapeDtypeStruct((rows, RANK), f32)),
        in_specs=[pl.BlockSpec(memory_space=pl.ANY)] * 3,
        out_specs=[pl.BlockSpec(memory_space=pltpu.VMEM)] * 2,
        scratch_shapes=[
            vmem((NX, rows, 2048), jnp.bfloat16),
            vmem((NX, rows, 2048), f32),
            vmem((NX, RANK, 2048), f32),
            vmem((NX, rows, 2048), f32),
            vmem((NX - 1, rows, 2048), f32),
            vmem((NY, NC, rows, 128), f32),
            vmem((NY - 1, NC, rows, 128), f32),
            vmem((NC, rows, 128), f32),
            vmem((NC, rows, 128), f32),
            vmem((NZ, NC, rows, 128), f32),
            vmem((8, 128), f32),
            vmem((NX, 8, 128), f32),
            vmem((8, 128), f32),
            vmem((NY, 8, 128), f32),
            vmem((NZ, NC, 8, 128), f32),
            vmem((128, 128), f32),
            pltpu.SemaphoreType.DMA((NX, 2, 3)),
            pltpu.SemaphoreType.DMA((64,)),
            pltpu.SemaphoreType.DMA((64,)),
        ],
        compiler_params=pltpu.CompilerParams(collective_id=0, has_side_effects=True, vmem_limit_bytes=24 * 2**20),
        name="reduce_factor_gather",
    )(grads[0], error[0], q_start.T)
    approx = jnp.dot(p_ortho, qt, precision=HIGHEST)
    merged = grads[0].astype(f32) + error[0]
    new_error = (merged - approx)[None]
    new_momentum = 0.9 * momentum + approx
    new_weight = (weight.astype(f32) - 0.5 * new_momentum).astype(jnp.bfloat16)
    return (new_error, new_momentum, new_weight, qt.T)


def solution(mesh):
    placed = (
        P("replica", "shard", None),
        P("replica", "shard", None),
        P("shard", None),
        P("shard", None),
        P(),
    )
    return jax.shard_map(
        on_device,
        mesh=mesh,
        in_specs=placed,
        out_specs=(P("replica", "shard", None), P("shard", None), P("shard", None), P()),
        check_vma=False,
    )
```

time: 425 us -> 63.7 us (0.15)
  waiting for transfers between devices: 269 us -> 0 us
  blocking collectives: 126 us -> 0 us
  Pallas kernels: 0 us -> 56.8 us
  between operations: 14.1 us -> 0.67 us
  other arithmetic: 7.98 us -> 0 us
  matrix products: 6.27 us -> 1.82 us
    psum x1 -> x0, waiting for transfers between devices: 269 us -> none  [on_device(): q_total = lax.psum(q_term, ('replica', 'shard'))]
    psum x2 -> x0, blocking collectives: 126 us -> none  [the longest x1 63.7 us: on_device(): p_sum = lax.psum(p_local, 'replica')]
    pallas_call x0 -> x1, Pallas kernels: none -> 56.8 us  [on_device(): pl.pallas_call(kernel, out_shape=(jax.ShapeDtypeStruct((RANK, D), f32), j...]
    another operation x5 -> x0, other arithmetic: 6.68 us -> none  [the longest x3 3.59 us: on_device(): factor = jnp.linalg.cholesky(gram)]
    dot_general x4 -> x1, matrix products: 6.12 us -> 1.82 us  [on_device(): approx = jnp.dot(p_ortho, qt, precision=HIGHEST)]
  transfers between devices with their start and end apart: 1 -> 0, of which waited for: 1 -> 0; matrix products, arithmetic and copies ran while one was open for 0% -> 0% of each run, Pallas kernels for 0% -> 0%
where the time goes in v1:
time: 63.7 us; the launch traced here: 63.4 us
  Pallas kernels  56.8 us (89%)
  local copies, waits for them, and re-layouts  4.19 us (7%)
  matrix products  1.82 us (3%)
  between operations  0.67 us (1%)
    pallas_call x1, Pallas kernels, on_device(): pl.pallas_call(kernel, out_shape=(jax.ShapeDtypeStruct((RANK, D), f32), j...  56.8 us
    unnamed x11, local copies, waits for them, and re-layouts  4.19 us
    dot_general x1, matrix products, on_device(): approx = jnp.dot(p_ortho, qt, precision=HIGHEST)  1.82 us

profile of v1, /device:TPU:1, one launch (start us, length us, event | category | flops | bytes accessed | tf_op | source)
XLA Modules:
  0.0 63.4 jit_solution(12432825136214108048)
XLA Ops:
  0.6 0.0 copy-start
  0.6 1.0 %copy-done = f32[1,16,8192]{2,1,0:T(8,128)S(1)} copy-done((f32[1,16,8192]{2,1,0:T(8,128)S(1)}, f32[1,16,8192]{2,1,0:T(8,128)}, u32[]{:S(2)}) %copy-start) | copy-done | bytes 524312
  1.7 0.0 copy-start.1
  1.7 1.2 %copy-done.1 = f32[8192,32]{0,1:T(8,128)S(1)} copy-done((f32[8192,32]{0,1:T(8,128)S(1)}, f32[8192,32]{0,1:T(8,128)}, u32[]{:S(2)}) %copy-start.1) | copy-done | bytes 1048600
  2.9 0.0 copy-start.2
  2.9 0.9 %copy-done.2 = bf16[1,16,8192]{2,1,0:T(8,128)(2,1)S(1)} copy-done((bf16[1,16,8192]{2,1,0:T(8,128)(2,1)S(1)}, bf16[1,16,8192]{2,1,0:T(8,128)(2,1)}, u32[]{:S(2)}) %copy-start.2) | copy-done | bytes 262168
  3.9 0.0 copy-start.3
  3.9 0.0 copy-start.4
  3.9 56.8 %reduce_factor_gather.1 = (f32[32,8192]{1,0:T(8,128)S(1)}, f32[16,32]{1,0:T(8,128)S(1)}) custom-call(bf16[16,8192]{1,0:T(8,128)(2,1)S(1)} %bitcast.13, f32[16,8192]{1,0:T(8,128)S(1)} %bitcast.11, f32[32,8192]{1,0:T(8,128)S(1)} %bitcast.12), custom_call_target="tpu_custom_call" | custom-call | tf_op jit(solution)/shard_map/reduce_factor_gather/pallas_call | solution.py:175
  60.6 0.0 copy-done.3
  60.6 0.0 copy-done.4
  60.6 1.8 %subtract_convert_fusion = (bf16[16,8192]{1,0:T(8,128)(2,1)}, f32[16,8192]{1,0:T(8,128)}, f32[1,16,8192]{2,1,0:T(8,128)}) fusion(bf16[16,8192]{1,0:T(8,128)(2,1)S(1)} %copy-done.4, f32[16,8192]{1,0:T(8,128)S(1)} %copy-done.3, f32[1,16,8192]{2,1,0:T(8,128)S(1)} %copy-done, bf16[1,16,8192]{2,1,0:T(8,128)(2,1)S(1)} %copy-done.2, ...), kind=kOutput, calls=%fused_computation | convolution fusion | flops 51511296 | bytes 3934208 | tf_op jit(solution)/shard_map/dot_general | solution.py:204
  62.5 1.0 %copy.10 = f32[8192,32]{0,1:T(8,128)} copy(f32[8192,32]{0,1:T(8,128)S(1)} %bitcast.10) | data formatting | bytes 2097152
Async XLA Ops:
  0.6 1.0 %copy-start = (f32[1,16,8192]{2,1,0:T(8,128)S(1)}, f32[1,16,8192]{2,1,0:T(8,128)}, u32[]{:S(2)}) copy-start(f32[1,16,8192]{2,1,0:T(8,128)} %param.6) | copy-start | bytes 1572868
  1.7 1.2 %copy-start.1 = (f32[8192,32]{0,1:T(8,128)S(1)}, f32[8192,32]{0,1:T(8,128)}, u32[]{:S(2)}) copy-start(f32[8192,32]{0,1:T(8,128)} %param.9) | copy-start | bytes 3145732
  2.9 0.9 %copy-start.2 = (bf16[1,16,8192]{2,1,0:T(8,128)(2,1)S(1)}, bf16[1,16,8192]{2,1,0:T(8,128)(2,1)}, u32[]{:S(2)}) copy-start(bf16[1,16,8192]{2,1,0:T(8,128)(2,1)} %param.5) | copy-start | bytes 786436
  3.9 56.8 %copy-start.3 = (f32[16,8192]{1,0:T(8,128)S(1)}, f32[16,8192]{1,0:T(8,128)}, u32[]{:S(2)}) copy-start(f32[16,8192]{1,0:T(8,128)} %param.7) | copy-start | bytes 1572868
  3.9 56.8 %copy-start.4 = (bf16[16,8192]{1,0:T(8,128)(2,1)S(1)}, bf16[16,8192]{1,0:T(8,128)(2,1)}, u32[]{:S(2)}) copy-start(bf16[16,8192]{1,0:T(8,128)(2,1)} %param.8) | copy-start | bytes 786436

commit v2 on v1

v2 whole, which is shorter than its diff:
```python
import jax
import jax.numpy as jnp
from jax import lax
from jax.experimental import pallas as pl
from jax.experimental.pallas import tpu as pltpu
from jax.sharding import PartitionSpec as P

MESH = pl.DeviceIdType.MESH
HIGHEST = lax.Precision.HIGHEST
NX, NY, NZ, NC = 4, 8, 8, 2
RANK = 32
D = 8192
NT = (((1,), (1,)), ((), ()))


def send(src, dst, send_sem, recv_sem, device):
    copy = pltpu.make_async_remote_copy(
        src_ref=src, dst_ref=dst, send_sem=send_sem, recv_sem=recv_sem,
        device_id=device, device_id_type=MESH,
    )
    copy.start()
    return copy


def factor_rows(gram, pt, steps):
    sub = lax.broadcasted_iota(jnp.int32, (RANK, 1), 0)
    for j in steps:
        col = gram[:, j:j + 1]
        r = lax.rsqrt(gram[j:j + 1, j:j + 1])
        f = jnp.where(sub > j, col * r, 0.0)
        grow = gram[j:j + 1, :] * r
        prow = pt[j:j + 1, :] * r
        gram = gram - f * grow
        pt = jnp.where(sub == j, prow, pt - f * prow)
    return gram, pt


def kernel(grads, error, qs, qt, po, gbuf, ebuf, qsv, mbuf, s1buf, relay, passed, s1sum, s2buf, msum, mpair, mall,
           ploc, pysum, pxbuf, pybuf, pall, oscr, load_sem, ssem, rsem):
    rep, shard = lax.axis_index("replica"), lax.axis_index("shard")
    x, y = lax.rem(rep, NX), lax.div(rep, NX)
    c, z = lax.rem(shard, NC), lax.div(shard, NC)

    def at_x(d):
        return (y * NX + lax.rem(x + d, NX), shard)

    def at_y(d):
        return (lax.rem(y + d, NY) * NX + x, shard)

    def at_z(d):
        return (rep, lax.rem(z + d, NZ) * NC + c)

    other = (rep, z * NC + (1 - c))

    barrier = pltpu.get_barrier_semaphore()
    partners = [at_x(d) for d in range(1, NX)] + [at_y(d) for d in range(1, NY)] + [at_z(d) for d in range(1, NZ)] + [other]
    for device in partners:
        pl.semaphore_signal(barrier, inc=1, device_id=device, device_id_type=MESH)

    slots = iter(range(128))
    started = []

    def go(src, dst, device):
        k = next(slots)
        copy = send(src, dst, ssem.at[k], rsem.at[k], device)
        started.append(copy)
        return copy

    ahead = [lax.rem(x + d, NX) for d in range(NX)]
    order = (2, 1, 3, 0)

    def load(src, dst, k, g):
        group = []
        for h in range(2):
            cols = pl.ds(pl.multiple_of(h * 4096 + g * 1024, 1024), 1024)
            cp = pltpu.make_async_copy(src.at[:, cols], dst.at[g, :, pl.ds(h * 1024, 1024)], load_sem.at[k, h])
            cp.start()
            group.append(cp)
        return group

    mloads = [load(grads, gbuf, i, ahead[d]) + load(error, ebuf, 4 + i, ahead[d]) for i, d in enumerate(order)]
    qloads = [load(qs, qsv, 8 + i, ahead[d]) for i, d in enumerate(order)]
    for i, d in enumerate(order):
        for cp in mloads[i]:
            cp.wait()
        mbuf[ahead[d]] = gbuf[ahead[d]].astype(jnp.float32) + ebuf[ahead[d]]

    lo, hi = pl.ds(0, 8), pl.ds(8, 8)
    pl.semaphore_wait(barrier, len(partners))
    right_relay = go(mbuf.at[ahead[2], lo], relay.at[0], at_x(1))
    left_relay = go(mbuf.at[ahead[2], hi], relay.at[1], at_x(3))
    right_own = go(mbuf.at[ahead[1], hi], s1buf.at[0, hi], at_x(1))
    left_own = go(mbuf.at[ahead[3], lo], s1buf.at[1, lo], at_x(3))

    p = None
    for i, d in enumerate(order):
        for cp in qloads[i]:
            cp.wait()
        t = lax.dot_general(mbuf[ahead[d]], qsv[ahead[d]], NT, precision=HIGHEST, preferred_element_type=jnp.float32)
        p = t if p is None else p + t
    packed = jnp.concatenate([p[0:8], p[8:16], jnp.zeros((8, 64), jnp.float32)], axis=1)
    ploc[...] = packed
    py = [go(ploc, pybuf.at[y], at_y(d)) for d in range(1, NY)]
    pybuf[y] = packed

    right_relay.wait_recv()
    passed[0] = mbuf[ahead[1], lo] + relay[0]
    right_sum = go(passed.at[0], s1buf.at[0, lo], at_x(1))
    left_relay.wait_recv()
    passed[1] = mbuf[ahead[3], hi] + relay[1]
    left_sum = go(passed.at[1], s1buf.at[1, hi], at_x(3))

    for cp in py:
        cp.wait_recv()
    packed = ((pybuf[0] + pybuf[1]) + (pybuf[2] + pybuf[3])) + ((pybuf[4] + pybuf[5]) + (pybuf[6] + pybuf[7]))
    pysum[...] = packed
    px = [go(pysum, pxbuf.at[x], at_x(d)) for d in range(1, NX)]
    pxbuf[x] = packed

    for cp in (right_own, left_own, right_sum, left_sum):
        cp.wait_recv()
    for k in range(NY):
        for h in range(2):
            cols = pl.ds(h * 1024 + k * 128, 128)
            s1sum[k, h] = mbuf[x, :, cols] + (s1buf[0, :, cols] + s1buf[1, :, cols])
    s2 = [go(s1sum.at[lax.rem(y + d, NY)], s2buf.at[d - 1], at_y(d)) for d in range(1, NY)]

    for cp in px:
        cp.wait_recv()
    pall[z, c] = (pxbuf[0] + pxbuf[1]) + (pxbuf[2] + pxbuf[3])
    pc = go(pall.at[z, c], pall.at[z, c], other)
    pc.wait_recv()
    pz = [go(pall.at[z], pall.at[z], at_z(d)) for d in range(1, NZ)]

    for cp in s2:
        cp.wait_recv()
    total = s1sum[y]
    for k in range(NY - 1):
        total = total + s2buf[k]
    msum[...] = total
    mpair[c] = msum[c]
    s3c = go(msum.at[1 - c], mpair.at[c], other)
    s3c.wait_recv()
    mall[z] = mpair[...]
    s3z = [go(mpair, mall.at[z], at_z(d)) for d in range(1, NZ)]

    for cp in pz:
        cp.wait_recv()
    pt = pall[...].reshape(128, 128).T
    p0, p1 = pt[0:RANK], pt[RANK:2 * RANK]
    gram = (lax.dot_general(p0, p0, NT, precision=HIGHEST, preferred_element_type=jnp.float32)
            + lax.dot_general(p1, p1, NT, precision=HIGHEST, preferred_element_type=jnp.float32))
    pt = jnp.concatenate([p0, p1], axis=1)
    gram, pt = factor_rows(gram, pt, range(RANK))
    ot = jnp.concatenate([pt[:, 0:128], pt[:, 128:256], jnp.zeros((64, 128), jnp.float32)], axis=0)
    oscr[...] = ot.T
    own = oscr[pl.ds(pl.multiple_of(shard * 8, 8), 8), :]
    po[0:8, :] = own[:, 0:RANK]
    po[8:16, :] = own[:, RANK:2 * RANK]

    for cp in s3z:
        cp.wait_recv()
    m0 = mall[:, :, 0:8, :].reshape(128, 128)
    m1 = mall[:, :, 8:16, :].reshape(128, 128)
    q = (jnp.dot(pt[:, 0:128], m0, precision=HIGHEST, preferred_element_type=jnp.float32)
         + jnp.dot(pt[:, 128:256], m1, precision=HIGHEST, preferred_element_type=jnp.float32)) * (1.0 / 32.0)

    def block(dx, dy):
        col = c * 4096 + lax.rem(x + dx, NX) * 1024 + lax.rem(y + dy, NY) * 128
        return pl.ds(pl.multiple_of(col, 128), 128)

    qt[:, block(0, 0)] = q

    def same(rows, cols, device):
        return go(qt.at[rows, cols], qt.at[rows, cols], device)

    every, top, low = pl.ds(0, RANK), pl.ds(0, RANK // 2), pl.ds(RANK // 2, RANK // 2)
    qy = {d: same(every, block(0, 0), at_y(d)) for d in (1, 7, 2, 6, 3, 5, 4)}
    arrivals = (0, 1, 7, 2, 6, 3, 5, 4)
    right, left, right_half, left_half = {}, {}, {}, {}
    for d in arrivals:
        if d:
            qy[d].wait_recv()
        right[d] = same(every, block(0, NY - d), at_x(1))
        left[d] = same(every, block(0, NY - d), at_x(3))
    group = pl.ds(pl.multiple_of(c * 4096 + x * 1024, 1024), 1024)
    qc = [same(every, group, other)]
    for d in arrivals:
        right[d].wait_recv()
        right_half[d] = same(top, block(3, NY - d), at_x(1))
        left[d].wait_recv()
        left_half[d] = same(low, block(1, NY - d), at_x(3))
    for dx in (1, 3, 2):
        if dx == 2:
            for d in arrivals:
                right_half[d].wait_recv()
                left_half[d].wait_recv()
        group = pl.ds(pl.multiple_of(c * 4096 + lax.rem(x + dx, NX) * 1024, 1024), 1024)
        qc.append(same(every, group, other))
    for cp in qc:
        cp.wait_recv()
    for cp in started:
        cp.wait_send()


def on_device(grads, error, momentum, weight, q_start):
    f32 = jnp.float32
    rows = grads.shape[1]
    vmem = pltpu.VMEM
    qt, p_ortho = pl.pallas_call(
        kernel,
        out_shape=(jax.ShapeDtypeStruct((RANK, D), f32), jax.ShapeDtypeStruct((rows, RANK), f32)),
        in_specs=[pl.BlockSpec(memory_space=pltpu.HBM)] * 3,
        out_specs=[pl.BlockSpec(memory_space=pltpu.VMEM)] * 2,
        scratch_shapes=[
            vmem((NX, rows, 2048), jnp.bfloat16),
            vmem((NX, rows, 2048), f32),
            vmem((NX, RANK, 2048), f32),
            vmem((NX, rows, 2048), f32),
            vmem((2, rows, 2048), f32),
            vmem((2, 8, 2048), f32),
            vmem((2, 8, 2048), f32),
            vmem((NY, NC, rows, 128), f32),
            vmem((NY - 1, NC, rows, 128), f32),
            vmem((NC, rows, 128), f32),
            vmem((NC, rows, 128), f32),
            vmem((NZ, NC, rows, 128), f32),
            vmem((8, 128), f32),
            vmem((8, 128), f32),
            vmem((NX, 8, 128), f32),
            vmem((NY, 8, 128), f32),
            vmem((NZ, NC, 8, 128), f32),
            vmem((128, 128), f32),
            pltpu.SemaphoreType.DMA((12, 2)),
            pltpu.SemaphoreType.DMA((96,)),
            pltpu.SemaphoreType.DMA((96,)),
        ],
        compiler_params=pltpu.CompilerParams(collective_id=0, has_side_effects=True, vmem_limit_bytes=24 * 2**20),
        name="reduce_factor_gather",
    )(*[pltpu.with_memory_space_constraint(a, pltpu.HBM) for a in (grads[0], error[0], q_start.T)])
    approx = jnp.dot(p_ortho, qt, precision=HIGHEST)
    merged = grads[0].astype(f32) + error[0]
    new_error = (merged - approx)[None]
    new_momentum = 0.9 * momentum + approx
    new_weight = (weight.astype(f32) - 0.5 * new_momentum).astype(jnp.bfloat16)
    return (new_error, new_momentum, new_weight, qt.T)


def solution(mesh):
    placed = (
        P("replica", "shard", None),
        P("replica", "shard", None),
        P("shard", None),
        P("shard", None),
        P(),
    )
    return jax.shard_map(
        on_device,
        mesh=mesh,
        in_specs=placed,
        out_specs=(P("replica", "shard", None), P("shard", None), P("shard", None), P()),
        check_vma=False,
    )
```

time: 63.7 us -> 54.1 us (0.85)
  Pallas kernels: 56.8 us -> 50.4 us
  local copies, waits for them, and re-layouts: 4.19 us -> 0.99 us
    pallas_call x1, Pallas kernels: 56.8 us -> 50.4 us  [on_device(): pl.pallas_call(kernel, out_shape=(jax.ShapeDtypeStruct((RANK, D), f32), j...]
    unnamed x11 -> x9, local copies, waits for them, and re-layouts: 4.19 us -> 0.99 us
where the time goes in v2:
time: 54.1 us; the launch traced here: 53.9 us
  Pallas kernels  50.4 us (93%)
  matrix products  1.82 us (3%)
  local copies, waits for them, and re-layouts  0.99 us (2%)
  between operations  0.7 us (1%)
    pallas_call x1, Pallas kernels, on_device(): pl.pallas_call(kernel, out_shape=(jax.ShapeDtypeStruct((RANK, D), f32), j...  50.4 us
    dot_general x1, matrix products, on_device(): approx = jnp.dot(p_ortho, qt, precision=HIGHEST)  1.82 us

profile of v2, /device:TPU:1, one launch (start us, length us, event | category | flops | bytes accessed | tf_op | source)
XLA Modules:
  0.0 53.9 jit_solution(13433615902744710731)
XLA Ops:
  0.6 0.0 copy-start
  0.6 0.0 copy-start.1
  0.7 0.0 copy-start.2
  0.7 0.0 copy-start.3
  0.7 50.4 %reduce_factor_gather.1 = (f32[32,8192]{1,0:T(8,128)S(1)}, f32[16,32]{1,0:T(8,128)S(1)}) custom-call(bf16[16,8192]{1,0:T(8,128)(2,1)} %bitcast.13, f32[16,8192]{1,0:T(8,128)} %bitcast.11, f32[32,8192]{1,0:T(8,128)} %bitcast.12), custom_call_target="tpu_custom_call" | custom-call | tf_op jit(solution)/shard_map/reduce_factor_gather/pallas_call | solution.py:210
  51.1 0.0 copy-done
  51.1 0.0 copy-done.1
  51.1 0.0 copy-done.2
  51.1 0.0 copy-done.3
  51.1 1.8 %subtract_convert_fusion = (bf16[16,8192]{1,0:T(8,128)(2,1)}, f32[16,8192]{1,0:T(8,128)}, f32[1,16,8192]{2,1,0:T(8,128)}) fusion(bf16[16,8192]{1,0:T(8,128)(2,1)S(1)} %copy-done.3, f32[16,8192]{1,0:T(8,128)S(1)} %copy-done.2, f32[1,16,8192]{2,1,0:T(8,128)S(1)} %copy-done, bf16[1,16,8192]{2,1,0:T(8,128)(2,1)S(1)} %copy-done.1, ...), kind=kOutput, calls=%fused_computation | convolution fusion | flops 51511296 | bytes 3934208 | tf_op jit(solution)/shard_map/dot_general | solution.py:241
  52.9 1.0 %copy.10 = f32[8192,32]{0,1:T(8,128)} copy(f32[8192,32]{0,1:T(8,128)S(1)} %bitcast.10) | data formatting | bytes 2097152
Async XLA Ops:
  0.6 50.4 %copy-start = (f32[1,16,8192]{2,1,0:T(8,128)S(1)}, f32[1,16,8192]{2,1,0:T(8,128)}, u32[]{:S(2)}) copy-start(f32[1,16,8192]{2,1,0:T(8,128)} %param.6) | copy-start | bytes 1572868
  0.6 50.4 %copy-start.1 = (bf16[1,16,8192]{2,1,0:T(8,128)(2,1)S(1)}, bf16[1,16,8192]{2,1,0:T(8,128)(2,1)}, u32[]{:S(2)}) copy-start(bf16[1,16,8192]{2,1,0:T(8,128)(2,1)} %param.5) | copy-start | bytes 786436
  0.7 50.4 %copy-start.2 = (f32[16,8192]{1,0:T(8,128)S(1)}, f32[16,8192]{1,0:T(8,128)}, u32[]{:S(2)}) copy-start(f32[16,8192]{1,0:T(8,128)} %param.7) | copy-start | bytes 1572868
  0.7 50.4 %copy-start.3 = (bf16[16,8192]{1,0:T(8,128)(2,1)S(1)}, bf16[16,8192]{1,0:T(8,128)(2,1)}, u32[]{:S(2)}) copy-start(bf16[16,8192]{1,0:T(8,128)(2,1)} %param.8) | copy-start | bytes 786436

commit v3 on v2

v3 whole, which is shorter than its diff:
```python
import jax
import jax.numpy as jnp
from jax import lax
from jax.experimental import pallas as pl
from jax.experimental.pallas import tpu as pltpu
from jax.sharding import PartitionSpec as P

MESH = pl.DeviceIdType.MESH
HIGHEST = lax.Precision.HIGHEST
NX, NY, NZ, NC = 4, 8, 8, 2
RANK = 32
D = 8192
NT = (((1,), (1,)), ((), ()))
FAR8, FAR4 = (4, 3, 5, 2, 6, 1, 7), (2, 1, 3)
ORDER = (0, 1, 7, 2, 6, 3, 4, 5)


def send(src, dst, send_sem, recv_sem, device):
    copy = pltpu.make_async_remote_copy(
        src_ref=src, dst_ref=dst, send_sem=send_sem, recv_sem=recv_sem,
        device_id=device, device_id_type=MESH,
    )
    copy.start()
    return copy


def factor_rows(gram, pt, steps):
    sub = lax.broadcasted_iota(jnp.int32, (RANK, 1), 0)
    for j in steps:
        col = gram[:, j:j + 1]
        r = lax.rsqrt(gram[j:j + 1, j:j + 1])
        f = jnp.where(sub > j, col * r, 0.0)
        grow = gram[j:j + 1, :] * r
        prow = pt[j:j + 1, :] * r
        gram = gram - f * grow
        pt = jnp.where(sub == j, prow, pt - f * prow)
    return gram, pt


def kernel(grads, error, qs, qb, po, gbuf, ebuf, qsv, mbuf, s1buf, relay, passed, s1sum, s2buf, msum, mall,
           ploc, pysum, pxbuf, pybuf, pall, oscr, load_sem, ssem, rsem):
    rep, shard = lax.axis_index("replica"), lax.axis_index("shard")
    x, y = lax.rem(rep, NX), lax.div(rep, NX)
    c, z = lax.rem(shard, NC), lax.div(shard, NC)

    def at_x(d):
        return (y * NX + lax.rem(x + d, NX), shard)

    def at_y(d):
        return (lax.rem(y + d, NY) * NX + x, shard)

    def at_z(d):
        return (rep, lax.rem(z + d, NZ) * NC + c)

    def at_zc(d):
        return (rep, lax.rem(z + d, NZ) * NC + (1 - c))

    other = at_zc(0)

    slots = iter(range(128))
    started = []

    def go(src, dst, device):
        k = next(slots)
        copy = send(src, dst, ssem.at[k], rsem.at[k], device)
        started.append(copy)
        return copy

    ahead = [lax.rem(x + d, NX) for d in range(NX)]
    order = (2, 1, 3, 0)

    def load(src, dst, k, g):
        cp = pltpu.make_async_copy(src.at[:, pl.ds(pl.multiple_of(g * 2048, 2048), 2048)], dst.at[g], load_sem.at[k])
        cp.start()
        return cp

    mloads = [(load(grads, gbuf, i, ahead[d]), load(error, ebuf, 4 + i, ahead[d])) for i, d in enumerate(order)]
    qloads = [load(qs, qsv, 8 + i, ahead[d]) for i, d in enumerate(order)]

    barrier = pltpu.get_barrier_semaphore()
    partners = [at(d) for d in FAR8 for at in (at_y, at_z, at_zc)] + [at_x(d) for d in FAR4] + [other]
    for device in partners:
        pl.semaphore_signal(barrier, inc=1, device_id=device, device_id_type=MESH)

    p = None
    for i, d in enumerate(order):
        for cp in mloads[i]:
            cp.wait()
        m = gbuf[ahead[d]].astype(jnp.float32) + ebuf[ahead[d]]
        mbuf[ahead[d]] = m
        qloads[i].wait()
        t = lax.dot_general(m, qsv[ahead[d]], NT, precision=HIGHEST, preferred_element_type=jnp.float32)
        p = t if p is None else p + t
    packed = jnp.concatenate([p[0:8], p[8:16], jnp.zeros((8, 64), jnp.float32)], axis=1)
    ploc[...] = packed

    lo, hi = pl.ds(0, 8), pl.ds(8, 8)
    pl.semaphore_wait(barrier, len(partners))
    right_relay = go(mbuf.at[ahead[2], lo], relay.at[0], at_x(1))
    left_relay = go(mbuf.at[ahead[2], hi], relay.at[1], at_x(3))
    right_own = go(mbuf.at[ahead[1], hi], s1buf.at[0, hi], at_x(1))
    left_own = go(mbuf.at[ahead[3], lo], s1buf.at[1, lo], at_x(3))

    py = [go(ploc, pybuf.at[y], at_y(d)) for d in FAR8]
    pybuf[y] = packed

    right_relay.wait_recv()
    passed[0] = mbuf[ahead[1], lo] + relay[0]
    right_sum = go(passed.at[0], s1buf.at[0, lo], at_x(1))
    left_relay.wait_recv()
    passed[1] = mbuf[ahead[3], hi] + relay[1]
    left_sum = go(passed.at[1], s1buf.at[1, hi], at_x(3))

    for cp in py:
        cp.wait_recv()
    packed = ((pybuf[0] + pybuf[1]) + (pybuf[2] + pybuf[3])) + ((pybuf[4] + pybuf[5]) + (pybuf[6] + pybuf[7]))
    pysum[...] = packed
    px = [go(pysum, pxbuf.at[x], at_x(d)) for d in FAR4]
    pxbuf[x] = packed

    for cp in (right_own, left_own, right_sum, left_sum):
        cp.wait_recv()
    for k in range(NY):
        for h in range(2):
            cols = pl.ds(h * 1024 + k * 128, 128)
            s1sum[k, h] = mbuf[x, :, cols] + (s1buf[0, :, cols] + s1buf[1, :, cols])
    s2 = [go(s1sum.at[lax.rem(y + d, NY)], s2buf.at[d - 1], at_y(d)) for d in FAR8]

    for cp in px:
        cp.wait_recv()
    pall[z, c] = (pxbuf[0] + pxbuf[1]) + (pxbuf[2] + pxbuf[3])
    pz = [go(pall.at[z, c], pall.at[z, c], at(d)) for d in FAR8 for at in (at_zc, at_z)] + [go(pall.at[z, c], pall.at[z, c], other)]

    for cp in s2:
        cp.wait_recv()
    total = s1sum[y]
    for k in range(NY - 1):
        total = total + s2buf[k]
    msum[...] = total
    mall[z, c] = msum[c]
    s3 = [go(msum.at[h], mall.at[z, c], at(d)) for d in FAR8 for h, at in ((1 - c, at_zc), (c, at_z))]
    s3.append(go(msum.at[1 - c], mall.at[z, c], other))

    for cp in pz:
        cp.wait_recv()
    pt = pall[...].reshape(128, 128).T
    p0, p1 = pt[0:RANK], pt[RANK:2 * RANK]
    gram = (lax.dot_general(p0, p0, NT, precision=HIGHEST, preferred_element_type=jnp.float32)
            + lax.dot_general(p1, p1, NT, precision=HIGHEST, preferred_element_type=jnp.float32))
    pt = jnp.concatenate([p0, p1], axis=1)
    gram, pt = factor_rows(gram, pt, range(RANK))
    ot = jnp.concatenate([pt[:, 0:128], pt[:, 128:256], jnp.zeros((64, 128), jnp.float32)], axis=0)
    oscr[...] = ot.T
    own = oscr[pl.ds(pl.multiple_of(shard * 8, 8), 8), :]
    po[0:8, :] = own[:, 0:RANK]
    po[8:16, :] = own[:, RANK:2 * RANK]

    for cp in s3:
        cp.wait_recv()
    m0 = mall[:, :, 0:8, :].reshape(128, 128)
    m1 = mall[:, :, 8:16, :].reshape(128, 128)
    q = (jnp.dot(pt[:, 0:128], m0, precision=HIGHEST, preferred_element_type=jnp.float32)
         + jnp.dot(pt[:, 128:256], m1, precision=HIGHEST, preferred_element_type=jnp.float32)) * (1.0 / 32.0)

    def same(g, start, rows, device):
        part = qb.at[g, c, pl.ds(start, rows)]
        return go(part, part, device)

    qb[x, c, 0:RANK] = q
    qy = {}
    for d in (4, 1, 7, 2, 6, 3, 5):
        qy[d] = go(qb.at[x, c, pl.ds(0, RANK)], qb.at[x, c, pl.ds(ORDER.index(d) * RANK, RANK)], at_y(d))
    batches = ((0, 32, 16), (32, 64, 32), (96, 64, 32), (160, 96, 48))
    right, left, halves, qc = [], [], [], []

    def pass_on(k):
        start, rows, _ = batches[k]
        for d in ORDER[start // RANK:(start + rows) // RANK]:
            if d:
                qy[d].wait_recv()
        right.append(same(x, start, rows, at_x(1)))
        left.append(same(x, start, rows, at_x(3)))

    def relay_on(k):
        start, rows, first = batches[k]
        right[k].wait_recv()
        halves.append(same(ahead[3], start, first, at_x(1)))
        left[k].wait_recv()
        halves.append(same(ahead[1], start + first, rows - first, at_x(3)))

    for k in range(4):
        pass_on(k)
    for k in range(4):
        relay_on(k)
    qc.append(same(x, 0, 256, other))
    qc.append(same(ahead[3], 0, 256, other))
    qc.append(same(ahead[1], 0, 256, other))
    for cp in halves:
        cp.wait_recv()
    qc.append(same(ahead[2], 0, 256, other))
    for cp in qc:
        cp.wait_recv()
    for cp in started:
        cp.wait_send()


def apply(po, qb, grads, error, momentum, weight, new_error, new_momentum, new_weight, q_next, qt, ebuf, mbuf, wbuf, sem):
    y = lax.div(lax.axis_index("replica"), NX)
    copies = []
    width = 2048
    for g in range(D // width):
        for c in range(NC):
            for k, d in enumerate(ORDER):
                col = g * width + c * 1024 + lax.rem(y + (NY - d), NY) * 128
                qt[:, pl.ds(pl.multiple_of(col, 128), 128)] = qb[g, c, k * RANK:(k + 1) * RANK]
        cols = pl.ds(g * width, width)
        cp = pltpu.make_async_copy(qt.at[:, cols], q_next.at[:, cols], sem.at[12 + g])
        cp.start()
        copies.append(cp)
        approx = jnp.dot(po[...], qt[:, cols], precision=HIGHEST, preferred_element_type=jnp.float32)
        ebuf[:, cols] = (grads[:, cols].astype(jnp.float32) + error[:, cols]) - approx
        moved = 0.9 * momentum[:, cols] + approx
        mbuf[:, cols] = moved
        wbuf[:, cols] = (weight[:, cols].astype(jnp.float32) - 0.5 * moved).astype(jnp.bfloat16)
        for k, (src, dst) in enumerate(((ebuf, new_error), (mbuf, new_momentum), (wbuf, new_weight))):
            cp = pltpu.make_async_copy(src.at[:, cols], dst.at[:, cols], sem.at[g * 3 + k])
            cp.start()
            copies.append(cp)
    for cp in copies:
        cp.wait()


def on_device(grads, error, momentum, weight, q_start):
    f32 = jnp.float32
    rows = grads.shape[1]
    vmem = pltpu.VMEM
    blocks, p_ortho = pl.pallas_call(
        kernel,
        out_shape=(jax.ShapeDtypeStruct((NX, NC, NY * RANK, 128), f32), jax.ShapeDtypeStruct((rows, RANK), f32)),
        in_specs=[pl.BlockSpec(memory_space=pltpu.HBM)] * 3,
        out_specs=[pl.BlockSpec(memory_space=pltpu.VMEM)] * 2,
        scratch_shapes=[
            vmem((NX, rows, 2048), jnp.bfloat16),
            vmem((NX, rows, 2048), f32),
            vmem((NX, RANK, 2048), f32),
            vmem((NX, rows, 2048), f32),
            vmem((2, rows, 2048), f32),
            vmem((2, 8, 2048), f32),
            vmem((2, 8, 2048), f32),
            vmem((NY, NC, rows, 128), f32),
            vmem((NY - 1, NC, rows, 128), f32),
            vmem((NC, rows, 128), f32),
            vmem((NZ, NC, rows, 128), f32),
            vmem((8, 128), f32),
            vmem((8, 128), f32),
            vmem((NX, 8, 128), f32),
            vmem((NY, 8, 128), f32),
            vmem((NZ, NC, 8, 128), f32),
            vmem((128, 128), f32),
            pltpu.SemaphoreType.DMA((12,)),
            pltpu.SemaphoreType.DMA((96,)),
            pltpu.SemaphoreType.DMA((96,)),
        ],
        compiler_params=pltpu.CompilerParams(collective_id=0, has_side_effects=True, vmem_limit_bytes=24 * 2**20),
        name="reduce_factor_gather",
    )(*[pltpu.with_memory_space_constraint(a, pltpu.HBM) for a in (grads[0], error[0], q_start.T)])
    new_error, new_momentum, new_weight, q_next = pl.pallas_call(
        apply,
        out_shape=(
            jax.ShapeDtypeStruct((rows, D), f32),
            jax.ShapeDtypeStruct((rows, D), f32),
            jax.ShapeDtypeStruct((rows, D), jnp.bfloat16),
            jax.ShapeDtypeStruct((RANK, D), f32),
        ),
        in_specs=[pl.BlockSpec(memory_space=pltpu.VMEM)] * 6,
        out_specs=[pl.BlockSpec(memory_space=pl.ANY)] * 4,
        scratch_shapes=[
            vmem((RANK, D), f32),
            vmem((rows, D), f32),
            vmem((rows, D), f32),
            vmem((rows, D), jnp.bfloat16),
            pltpu.SemaphoreType.DMA((16,)),
        ],
        compiler_params=pltpu.CompilerParams(vmem_limit_bytes=24 * 2**20),
        name="apply",
    )(p_ortho, blocks, grads[0], error[0], momentum, weight)
    return (new_error[None], new_momentum, new_weight, q_next.T)


def solution(mesh):
    placed = (
        P("replica", "shard", None),
        P("replica", "shard", None),
        P("shard", None),
        P("shard", None),
        P(),
    )
    return jax.shard_map(
        on_device,
        mesh=mesh,
        in_specs=placed,
        out_specs=(P("replica", "shard", None), P("shard", None), P("shard", None), P()),
        check_vma=False,
    )
```

time: 54.1 us -> 51.8 us (0.957)
  matrix products: 1.82 us -> 0 us
  local copies, waits for them, and re-layouts: 0.99 us -> 0.02 us
    dot_general x1 -> x0, matrix products: 1.82 us -> none  [on_device(): approx = jnp.dot(p_ortho, qt, precision=HIGHEST)]
    unnamed x9 -> x8, local copies, waits for them, and re-layouts: 0.99 us -> 0.02 us
    pallas_call x1 -> x2, Pallas kernels: 50.4 us -> 50.9 us  [the longest x1 49.1 us: on_device(): pl.pallas_call(kernel, out_shape=(jax.ShapeDtypeStruct((NX, NC, NY * RANK...]
where the time goes in v3:
time: 51.8 us; the launch traced here: 51.6 us
  Pallas kernels  50.9 us (98%)
  between operations  0.7 us (1%)
    pallas_call x1, Pallas kernels, on_device(): pl.pallas_call(kernel, out_shape=(jax.ShapeDtypeStruct((NX, NC, NY * RANK...  49.1 us
    pallas_call x1, Pallas kernels, on_device(): pl.pallas_call(apply, out_shape=(jax.ShapeDtypeStruct((rows, D), f32), ja...  1.82 us

profile of v3, /device:TPU:1, one launch (start us, length us, event | category | flops | bytes accessed | tf_op | source)
XLA Modules:
  0.0 51.6 jit_solution(8809462779882336951)
XLA Ops:
  0.6 0.0 copy-start
  0.6 0.0 copy-start.1
  0.7 0.0 copy-start.2
  0.7 0.0 copy-start.3
  0.7 49.1 %reduce_factor_gather.1 = (f32[4,2,256,128]{3,2,1,0:T(8,128)S(1)}, f32[16,32]{1,0:T(8,128)S(1)}) custom-call(bf16[16,8192]{1,0:T(8,128)(2,1)} %bitcast.7, f32[16,8192]{1,0:T(8,128)} %bitcast.5, f32[32,8192]{1,0:T(8,128)} %bitcast.9), custom_call_target="tpu_custom_call" | custom-call | tf_op jit(solution)/shard_map/reduce_factor_gather/pallas_call | solution.py:237
  49.8 0.0 copy-done
  49.8 0.0 copy-done.1
  49.8 0.0 copy-done.2
  49.8 0.0 copy-done.3
  49.8 1.8 %apply.1 = (f32[16,8192]{1,0:T(8,128)}, f32[16,8192]{1,0:T(8,128)}, bf16[16,8192]{1,0:T(8,128)(2,1)}, f32[32,8192]{1,0:T(8,128)}) custom-call(f32[16,32]{1,0:T(8,128)S(1)} %get-tuple-element.10.po, f32[4,2,256,128]{3,2,1,0:T(8,128)S(1)} %get-tuple-element.11.qb, bf16[16,8192]{1,0:T(8,128)(2,1)S(1)} %bitcast.8, f32[16,8192]{1,0:T(8,128)S(1)} %bitcast.6, ...), custom_call_target="tpu_custom_call" | custom-call | tf_op jit(solution)/shard_map/apply/pallas_call | solution.py:267
Async XLA Ops:
  0.6 49.1 %copy-start = (f32[1,16,8192]{2,1,0:T(8,128)S(1)}, f32[1,16,8192]{2,1,0:T(8,128)}, u32[]{:S(2)}) copy-start(f32[1,16,8192]{2,1,0:T(8,128)} %param.6) | copy-start | bytes 1572868
  0.6 49.1 %copy-start.1 = (bf16[1,16,8192]{2,1,0:T(8,128)(2,1)S(1)}, bf16[1,16,8192]{2,1,0:T(8,128)(2,1)}, u32[]{:S(2)}) copy-start(bf16[1,16,8192]{2,1,0:T(8,128)(2,1)} %param.5) | copy-start | bytes 786436
  0.7 49.1 %copy-start.2 = (f32[16,8192]{1,0:T(8,128)S(1)}, f32[16,8192]{1,0:T(8,128)}, u32[]{:S(2)}) copy-start(f32[16,8192]{1,0:T(8,128)} %momentum.1) | copy-start | bytes 1572868
  0.7 49.1 %copy-start.3 = (bf16[16,8192]{1,0:T(8,128)(2,1)S(1)}, bf16[16,8192]{1,0:T(8,128)(2,1)}, u32[]{:S(2)}) copy-start(bf16[16,8192]{1,0:T(8,128)(2,1)} %weight.1) | copy-start | bytes 786436

commit v4 on v3

--- a/solution.py
+++ b/solution.py
@@ -74,42 +74,48 @@
         cp.start()
         return cp
 
+    barrier = pltpu.get_barrier_semaphore()
+    partners = [at(d) for d in FAR8 for at in (at_y, at_z, at_zc)] + [other]
+    partners = partners[:9] + [at_x(d) for d in FAR4] + partners[9:]
+
+    def signal(some):
+        for device in some:
+            pl.semaphore_signal(barrier, inc=1, device_id=device, device_id_type=MESH)
+
+    signal(partners[:10])
     mloads = [(load(grads, gbuf, i, ahead[d]), load(error, ebuf, 4 + i, ahead[d])) for i, d in enumerate(order)]
+    signal(partners[10:])
     qloads = [load(qs, qsv, 8 + i, ahead[d]) for i, d in enumerate(order)]
 
-    barrier = pltpu.get_barrier_semaphore()
-    partners = [at(d) for d in FAR8 for at in (at_y, at_z, at_zc)] + [at_x(d) for d in FAR4] + [other]
-    for device in partners:
-        pl.semaphore_signal(barrier, inc=1, device_id=device, device_id_type=MESH)
-
-    p = None
     for i, d in enumerate(order):
         for cp in mloads[i]:
             cp.wait()
-        m = gbuf[ahead[d]].astype(jnp.float32) + ebuf[ahead[d]]
-        mbuf[ahead[d]] = m
+        mbuf[ahead[d]] = gbuf[ahead[d]].astype(jnp.float32) + ebuf[ahead[d]]
+
+    lo, hi = pl.ds(0, 8), pl.ds(8, 8)
+    pl.semaphore_wait(barrier, len(partners))
+    parts = [pl.ds(k * 1024, 1024) for k in range(2)]
+    relays = [(go(mbuf.at[ahead[2], lo, part], relay.at[0, :, part], at_x(1)),
+               go(mbuf.at[ahead[2], hi, part], relay.at[1, :, part], at_x(3))) for part in parts]
+    right_own = go(mbuf.at[ahead[1], hi], s1buf.at[0, hi], at_x(1))
+    left_own = go(mbuf.at[ahead[3], lo], s1buf.at[1, lo], at_x(3))
+
+    p = None
+    for i, d in enumerate(order):
         qloads[i].wait()
-        t = lax.dot_general(m, qsv[ahead[d]], NT, precision=HIGHEST, preferred_element_type=jnp.float32)
+        t = lax.dot_general(mbuf[ahead[d]], qsv[ahead[d]], NT, precision=HIGHEST, preferred_element_type=jnp.float32)
         p = t if p is None else p + t
     packed = jnp.concatenate([p[0:8], p[8:16], jnp.zeros((8, 64), jnp.float32)], axis=1)
     ploc[...] = packed
-
-    lo, hi = pl.ds(0, 8), pl.ds(8, 8)
-    pl.semaphore_wait(barrier, len(partners))
-    right_relay = go(mbuf.at[ahead[2], lo], relay.at[0], at_x(1))
-    left_relay = go(mbuf.at[ahead[2], hi], relay.at[1], at_x(3))
-    right_own = go(mbuf.at[ahead[1], hi], s1buf.at[0, hi], at_x(1))
-    left_own = go(mbuf.at[ahead[3], lo], s1buf.at[1, lo], at_x(3))
-
     py = [go(ploc, pybuf.at[y], at_y(d)) for d in FAR8]
     pybuf[y] = packed
 
-    right_relay.wait_recv()
-    passed[0] = mbuf[ahead[1], lo] + relay[0]
-    right_sum = go(passed.at[0], s1buf.at[0, lo], at_x(1))
-    left_relay.wait_recv()
-    passed[1] = mbuf[ahead[3], hi] + relay[1]
-    left_sum = go(passed.at[1], s1buf.at[1, hi], at_x(3))
+    sums = []
+    for k, part in enumerate(parts):
+        for side, (g, rows, device) in enumerate(((ahead[1], lo, at_x(1)), (ahead[3], hi, at_x(3)))):
+            relays[k][side].wait_recv()
+            passed[side, :, part] = mbuf[g, rows, part] + relay[side, :, part]
+            sums.append(go(passed.at[side, :, part], s1buf.at[side, rows, part], device))
 
     for cp in py:
         cp.wait_recv()
@@ -118,7 +124,7 @@
     px = [go(pysum, pxbuf.at[x], at_x(d)) for d in FAR4]
     pxbuf[x] = packed
 
-    for cp in (right_own, left_own, right_sum, left_sum):
+    for cp in [right_own, left_own] + sums:
         cp.wait_recv()
     for k in range(NY):
         for h in range(2):
@@ -168,36 +174,21 @@
 
     qb[x, c, 0:RANK] = q
     qy = {}
-    for d in (4, 1, 7, 2, 6, 3, 5):
+    for d in (1, 7, 2, 6, 4, 3, 5):
         qy[d] = go(qb.at[x, c, pl.ds(0, RANK)], qb.at[x, c, pl.ds(ORDER.index(d) * RANK, RANK)], at_y(d))
-    batches = ((0, 32, 16), (32, 64, 32), (96, 64, 32), (160, 96, 48))
-    right, left, halves, qc = [], [], [], []
-
-    def pass_on(k):
-        start, rows, _ = batches[k]
+    batches = ((0, 32), (32, 64), (96, 64), (160, 96))
+    qx = []
+    for start, rows in batches:
         for d in ORDER[start // RANK:(start + rows) // RANK]:
             if d:
                 qy[d].wait_recv()
-        right.append(same(x, start, rows, at_x(1)))
-        left.append(same(x, start, rows, at_x(3)))
-
-    def relay_on(k):
-        start, rows, first = batches[k]
-        right[k].wait_recv()
-        halves.append(same(ahead[3], start, first, at_x(1)))
-        left[k].wait_recv()
-        halves.append(same(ahead[1], start + first, rows - first, at_x(3)))
-
-    for k in range(4):
-        pass_on(k)
-    for k in range(4):
-        relay_on(k)
-    qc.append(same(x, 0, 256, other))
-    qc.append(same(ahead[3], 0, 256, other))
-    qc.append(same(ahead[1], 0, 256, other))
-    for cp in halves:
-        cp.wait_recv()
-    qc.append(same(ahead[2], 0, 256, other))
+        qx.append([same(x, start, rows, at_x(d)) for d in FAR4])
+    qc = [same(x, 0, 256, other)]
+    for some, start, rows in ((qx[:3], 0, 160), (qx[3:], 160, 96)):
+        for k, d in enumerate(FAR4):
+            for sent in some:
+                sent[k].wait_recv()
+            qc.append(same(ahead[NX - d], start, rows, other))
     for cp in qc:
         cp.wait_recv()
     for cp in started:

time: 51.8 us -> 49.6 us (0.958)
  Pallas kernels: 50.9 us -> 48.7 us
    pallas_call x1, Pallas kernels: 49.1 us -> 46.9 us  [on_device(): pl.pallas_call(kernel, out_shape=(jax.ShapeDtypeStruct((NX, NC, NY * RANK...]
where the time goes in v4:
time: 49.6 us; the launch traced here: 49.5 us
  Pallas kernels  48.7 us (98%)
  between operations  0.7 us (1%)
    pallas_call x1, Pallas kernels, on_device(): pl.pallas_call(kernel, out_shape=(jax.ShapeDtypeStruct((NX, NC, NY * RANK...  46.9 us
    pallas_call x1, Pallas kernels, on_device(): pl.pallas_call(apply, out_shape=(jax.ShapeDtypeStruct((rows, D), f32), ja...  1.82 us

profile of v4, /device:TPU:1, one launch (start us, length us, event | category | flops | bytes accessed | tf_op | source)
XLA Modules:
  0.0 49.5 jit_solution(15948199042659447298)
XLA Ops:
  0.6 0.0 copy-start
  0.6 0.0 copy-start.1
  0.7 0.0 copy-start.2
  0.7 0.0 copy-start.3
  0.7 46.9 %reduce_factor_gather.1 = (f32[4,2,256,128]{3,2,1,0:T(8,128)S(1)}, f32[16,32]{1,0:T(8,128)S(1)}) custom-call(bf16[16,8192]{1,0:T(8,128)(2,1)} %bitcast.7, f32[16,8192]{1,0:T(8,128)} %bitcast.5, f32[32,8192]{1,0:T(8,128)} %bitcast.9), custom_call_target="tpu_custom_call" | custom-call | tf_op jit(solution)/shard_map/reduce_factor_gather/pallas_call | solution.py:228
  47.6 0.0 copy-done
  47.6 0.0 copy-done.1
  47.6 0.0 copy-done.2
  47.6 0.0 copy-done.3
  47.6 1.8 %apply.1 = (f32[16,8192]{1,0:T(8,128)}, f32[16,8192]{1,0:T(8,128)}, bf16[16,8192]{1,0:T(8,128)(2,1)}, f32[32,8192]{1,0:T(8,128)}) custom-call(f32[16,32]{1,0:T(8,128)S(1)} %get-tuple-element.10.po, f32[4,2,256,128]{3,2,1,0:T(8,128)S(1)} %get-tuple-element.11.qb, bf16[16,8192]{1,0:T(8,128)(2,1)S(1)} %bitcast.8, f32[16,8192]{1,0:T(8,128)S(1)} %bitcast.6, ...), custom_call_target="tpu_custom_call" | custom-call | tf_op jit(solution)/shard_map/apply/pallas_call | solution.py:258
Async XLA Ops:
  0.6 47.0 %copy-start = (f32[1,16,8192]{2,1,0:T(8,128)S(1)}, f32[1,16,8192]{2,1,0:T(8,128)}, u32[]{:S(2)}) copy-start(f32[1,16,8192]{2,1,0:T(8,128)} %param.6) | copy-start | bytes 1572868
  0.6 47.0 %copy-start.1 = (bf16[1,16,8192]{2,1,0:T(8,128)(2,1)S(1)}, bf16[1,16,8192]{2,1,0:T(8,128)(2,1)}, u32[]{:S(2)}) copy-start(bf16[1,16,8192]{2,1,0:T(8,128)(2,1)} %param.5) | copy-start | bytes 786436
  0.7 47.0 %copy-start.2 = (f32[16,8192]{1,0:T(8,128)S(1)}, f32[16,8192]{1,0:T(8,128)}, u32[]{:S(2)}) copy-start(f32[16,8192]{1,0:T(8,128)} %momentum.1) | copy-start | bytes 1572868
  0.7 47.0 %copy-start.3 = (bf16[16,8192]{1,0:T(8,128)(2,1)S(1)}, bf16[16,8192]{1,0:T(8,128)(2,1)}, u32[]{:S(2)}) copy-start(bf16[16,8192]{1,0:T(8,128)(2,1)} %weight.1) | copy-start | bytes 786436

commit v5 on v4

--- a/solution.py
+++ b/solution.py
@@ -37,7 +37,7 @@
     return gram, pt
 
 
-def kernel(grads, error, qs, qb, po, gbuf, ebuf, qsv, mbuf, s1buf, relay, passed, s1sum, s2buf, msum, mall,
+def kernel(grads, error, qs, qb, po, mbuf, gbuf, ebuf, qsv, s1buf, relay, passed, s1sum, s2buf, msum, mall,
            ploc, pysum, pxbuf, pybuf, pall, oscr, load_sem, ssem, rsem):
     rep, shard = lax.axis_index("replica"), lax.axis_index("shard")
     x, y = lax.rem(rep, NX), lax.div(rep, NX)
@@ -155,33 +155,32 @@
             + lax.dot_general(p1, p1, NT, precision=HIGHEST, preferred_element_type=jnp.float32))
     pt = jnp.concatenate([p0, p1], axis=1)
     gram, pt = factor_rows(gram, pt, range(RANK))
+    for cp in s3:
+        cp.wait_recv()
+    m = jnp.concatenate([mall[:, :, 0:8, :].reshape(128, 128), mall[:, :, 8:16, :].reshape(128, 128)], axis=0)
+    q = jnp.dot(pt, m, precision=HIGHEST, preferred_element_type=jnp.float32) * (1.0 / 32.0)
+
+    def same(g, start, rows, device):
+        part = qb.at[g, c, pl.ds(start, rows)]
+        return go(part, part, device)
+
+    qb[x, c, 0:RANK] = q
+    before = len(started)
+    qy = {}
+    for d in (1, 7, 2, 6, 4, 3, 5):
+        qy[d] = go(qb.at[x, c, pl.ds(0, RANK)], qb.at[x, c, pl.ds(ORDER.index(d) * RANK, RANK)], at_y(d))
+    batches = ((0, 32), (32, 64), (96, 64), (160, 96))
+    qx = [[same(x, 0, RANK, at_x(d)) for d in FAR4]]
     ot = jnp.concatenate([pt[:, 0:128], pt[:, 128:256], jnp.zeros((64, 128), jnp.float32)], axis=0)
     oscr[...] = ot.T
     own = oscr[pl.ds(pl.multiple_of(shard * 8, 8), 8), :]
     po[0:8, :] = own[:, 0:RANK]
     po[8:16, :] = own[:, RANK:2 * RANK]
-
-    for cp in s3:
-        cp.wait_recv()
-    m0 = mall[:, :, 0:8, :].reshape(128, 128)
-    m1 = mall[:, :, 8:16, :].reshape(128, 128)
-    q = (jnp.dot(pt[:, 0:128], m0, precision=HIGHEST, preferred_element_type=jnp.float32)
-         + jnp.dot(pt[:, 128:256], m1, precision=HIGHEST, preferred_element_type=jnp.float32)) * (1.0 / 32.0)
-
-    def same(g, start, rows, device):
-        part = qb.at[g, c, pl.ds(start, rows)]
-        return go(part, part, device)
-
-    qb[x, c, 0:RANK] = q
-    qy = {}
-    for d in (1, 7, 2, 6, 4, 3, 5):
-        qy[d] = go(qb.at[x, c, pl.ds(0, RANK)], qb.at[x, c, pl.ds(ORDER.index(d) * RANK, RANK)], at_y(d))
-    batches = ((0, 32), (32, 64), (96, 64), (160, 96))
-    qx = []
-    for start, rows in batches:
+    for cp in started[:before]:
+        cp.wait_send()
+    for start, rows in batches[1:]:
         for d in ORDER[start // RANK:(start + rows) // RANK]:
-            if d:
-                qy[d].wait_recv()
+            qy[d].wait_recv()
         qx.append([same(x, start, rows, at_x(d)) for d in FAR4])
     qc = [same(x, 0, 256, other)]
     for some, start, rows in ((qx[:3], 0, 160), (qx[3:], 160, 96)):
@@ -189,13 +188,14 @@
             for sent in some:
                 sent[k].wait_recv()
             qc.append(same(ahead[NX - d], start, rows, other))
+    for cp in started[before:-1]:
+        cp.wait_send()
     for cp in qc:
         cp.wait_recv()
-    for cp in started:
-        cp.wait_send()
-
-
-def apply(po, qb, grads, error, momentum, weight, new_error, new_momentum, new_weight, q_next, qt, ebuf, mbuf, wbuf, sem):
+    started[-1].wait_send()
+
+
+def apply(po, qb, merged, momentum, weight, new_error, new_momentum, new_weight, q_next, qt, ebuf, mbuf, wbuf, sem):
     y = lax.div(lax.axis_index("replica"), NX)
     copies = []
     width = 2048
@@ -209,7 +209,7 @@
         cp.start()
         copies.append(cp)
         approx = jnp.dot(po[...], qt[:, cols], precision=HIGHEST, preferred_element_type=jnp.float32)
-        ebuf[:, cols] = (grads[:, cols].astype(jnp.float32) + error[:, cols]) - approx
+        ebuf[:, cols] = merged[g] - approx
         moved = 0.9 * momentum[:, cols] + approx
         mbuf[:, cols] = moved
         wbuf[:, cols] = (weight[:, cols].astype(jnp.float32) - 0.5 * moved).astype(jnp.bfloat16)
@@ -225,16 +225,16 @@
     f32 = jnp.float32
     rows = grads.shape[1]
     vmem = pltpu.VMEM
-    blocks, p_ortho = pl.pallas_call(
+    blocks, p_ortho, merged = pl.pallas_call(
         kernel,
-        out_shape=(jax.ShapeDtypeStruct((NX, NC, NY * RANK, 128), f32), jax.ShapeDtypeStruct((rows, RANK), f32)),
+        out_shape=(jax.ShapeDtypeStruct((NX, NC, NY * RANK, 128), f32), jax.ShapeDtypeStruct((rows, RANK), f32),
+                   jax.ShapeDtypeStruct((NX, rows, 2048), f32)),
         in_specs=[pl.BlockSpec(memory_space=pltpu.HBM)] * 3,
-        out_specs=[pl.BlockSpec(memory_space=pltpu.VMEM)] * 2,
+        out_specs=[pl.BlockSpec(memory_space=pltpu.VMEM)] * 3,
         scratch_shapes=[
             vmem((NX, rows, 2048), jnp.bfloat16),
             vmem((NX, rows, 2048), f32),
             vmem((NX, RANK, 2048), f32),
-            vmem((NX, rows, 2048), f32),
             vmem((2, rows, 2048), f32),
             vmem((2, 8, 2048), f32),
             vmem((2, 8, 2048), f32),
@@ -263,7 +263,7 @@
             jax.ShapeDtypeStruct((rows, D), jnp.bfloat16),
             jax.ShapeDtypeStruct((RANK, D), f32),
         ),
-        in_specs=[pl.BlockSpec(memory_space=pltpu.VMEM)] * 6,
+        in_specs=[pl.BlockSpec(memory_space=pltpu.VMEM)] * 5,
         out_specs=[pl.BlockSpec(memory_space=pl.ANY)] * 4,
         scratch_shapes=[
             vmem((RANK, D), f32),
@@ -274,7 +274,7 @@
         ],
         compiler_params=pltpu.CompilerParams(vmem_limit_bytes=24 * 2**20),
         name="apply",
-    )(p_ortho, blocks, grads[0], error[0], momentum, weight)
+    )(p_ortho, blocks, merged, momentum, weight)
     return (new_error[None], new_momentum, new_weight, q_next.T)
 
 

time: 49.6 us -> 49.1 us (0.990)
  no operation moved by 1% of the time
where the time goes in v5:
time: 49.1 us; the launch traced here: 49 us
  Pallas kernels  48.3 us (98%)
  between operations  0.67 us (1%)
    pallas_call x1, Pallas kernels, on_device(): pl.pallas_call(kernel, out_shape=(jax.ShapeDtypeStruct((NX, NC, NY * RANK...  46.5 us
    pallas_call x1, Pallas kernels, on_device(): pl.pallas_call(apply, out_shape=(jax.ShapeDtypeStruct((rows, D), f32), ja...  1.81 us

profile of v5, /device:TPU:1, one launch (start us, length us, event | category | flops | bytes accessed | tf_op | source)
XLA Modules:
  0.0 49.0 jit_solution(14045624830406253663)
XLA Ops:
  0.6 0.0 copy-start
  0.6 0.0 copy-start.1
  0.7 46.5 %reduce_factor_gather.1 = (f32[4,2,256,128]{3,2,1,0:T(8,128)S(1)}, f32[16,32]{1,0:T(8,128)S(1)}, f32[4,16,2048]{2,1,0:T(8,128)S(1)}) custom-call(bf16[16,8192]{1,0:T(8,128)(2,1)} %bitcast.7, f32[16,8192]{1,0:T(8,128)} %bitcast.6, f32[32,8192]{1,0:T(8,128)} %bitcast.5), custom_call_target="tpu_custom_call" | custom-call | tf_op jit(solution)/shard_map/reduce_factor_gather/pallas_call | solution.py:228
  47.2 0.0 copy-done
  47.2 0.0 copy-done.1
  47.2 1.8 %apply.1 = (f32[16,8192]{1,0:T(8,128)}, f32[16,8192]{1,0:T(8,128)}, bf16[16,8192]{1,0:T(8,128)(2,1)}, f32[32,8192]{1,0:T(8,128)}) custom-call(f32[16,32]{1,0:T(8,128)S(1)} %get-tuple-element.11.po, f32[4,2,256,128]{3,2,1,0:T(8,128)S(1)} %get-tuple-element.12.qb, f32[4,16,2048]{2,1,0:T(8,128)S(1)} %get-tuple-element.13.merged, f32[16,8192]{1,0:T(8,128)S(1)} %copy-done, ...), custom_call_target="tpu_custom_call" | custom-call | tf_op jit(solution)/shard_map/apply/pallas_call | solution.py:258
Async XLA Ops:
  0.6 46.5 %copy-start = (f32[16,8192]{1,0:T(8,128)S(1)}, f32[16,8192]{1,0:T(8,128)}, u32[]{:S(2)}) copy-start(f32[16,8192]{1,0:T(8,128)} %momentum.1) | copy-start | bytes 1572868
  0.6 46.5 %copy-start.1 = (bf16[16,8192]{1,0:T(8,128)(2,1)S(1)}, bf16[16,8192]{1,0:T(8,128)(2,1)}, u32[]{:S(2)}) copy-start(bf16[16,8192]{1,0:T(8,128)(2,1)} %weight.1) | copy-start | bytes 786436

commit v6 on v5

--- a/solution.py
+++ b/solution.py
@@ -195,8 +195,17 @@
     started[-1].wait_send()
 
 
+def thirds(a):
+    high = a.astype(jnp.bfloat16)
+    rest = a - high.astype(jnp.float32)
+    middle = rest.astype(jnp.bfloat16)
+    return high, middle, (rest - middle.astype(jnp.float32)).astype(jnp.bfloat16)
+
+
 def apply(po, qb, merged, momentum, weight, new_error, new_momentum, new_weight, q_next, qt, ebuf, mbuf, wbuf, sem):
     y = lax.div(lax.axis_index("replica"), NX)
+    high, middle, low = thirds(po[...])
+    left = jnp.concatenate([high, high, high, middle, middle, low], axis=1)
     copies = []
     width = 2048
     for g in range(D // width):
@@ -208,7 +217,9 @@
         cp = pltpu.make_async_copy(qt.at[:, cols], q_next.at[:, cols], sem.at[12 + g])
         cp.start()
         copies.append(cp)
-        approx = jnp.dot(po[...], qt[:, cols], precision=HIGHEST, preferred_element_type=jnp.float32)
+        high, middle, low = thirds(qt[:, cols])
+        right = jnp.concatenate([high, middle, low, high, middle, high], axis=0)
+        approx = jnp.dot(left, right, preferred_element_type=jnp.float32)
         ebuf[:, cols] = merged[g] - approx
         moved = 0.9 * momentum[:, cols] + approx
         mbuf[:, cols] = moved

time: 49.1 us -> 49 us (level)
  no operation moved by 1% of the time
where the time goes in v6:
time: 49 us; the launch traced here: 48.9 us
  Pallas kernels  48.2 us (98%)
  between operations  0.67 us (1%)
    pallas_call x1, Pallas kernels, on_device(): pl.pallas_call(kernel, out_shape=(jax.ShapeDtypeStruct((NX, NC, NY * RANK...  46.5 us
    pallas_call x1, Pallas kernels, on_device(): pl.pallas_call(apply, out_shape=(jax.ShapeDtypeStruct((rows, D), f32), ja...  1.71 us

profile of v6, /device:TPU:1, one launch (start us, length us, event | category | flops | bytes accessed | tf_op | source)
XLA Modules:
  0.0 48.9 jit_solution(15408641385300728488)
XLA Ops:
  0.6 0.0 copy-start
  0.6 0.0 copy-start.1
  0.7 46.5 %reduce_factor_gather.1 = (f32[4,2,256,128]{3,2,1,0:T(8,128)S(1)}, f32[16,32]{1,0:T(8,128)S(1)}, f32[4,16,2048]{2,1,0:T(8,128)S(1)}) custom-call(bf16[16,8192]{1,0:T(8,128)(2,1)} %bitcast.7, f32[16,8192]{1,0:T(8,128)} %bitcast.6, f32[32,8192]{1,0:T(8,128)} %bitcast.5), custom_call_target="tpu_custom_call" | custom-call | tf_op jit(solution)/shard_map/reduce_factor_gather/pallas_call | solution.py:239
  47.2 0.0 copy-done
  47.2 0.0 copy-done.1
  47.2 1.7 %apply.1 = (f32[16,8192]{1,0:T(8,128)}, f32[16,8192]{1,0:T(8,128)}, bf16[16,8192]{1,0:T(8,128)(2,1)}, f32[32,8192]{1,0:T(8,128)}) custom-call(f32[16,32]{1,0:T(8,128)S(1)} %get-tuple-element.11.po, f32[4,2,256,128]{3,2,1,0:T(8,128)S(1)} %get-tuple-element.12.qb, f32[4,16,2048]{2,1,0:T(8,128)S(1)} %get-tuple-element.13.merged, f32[16,8192]{1,0:T(8,128)S(1)} %copy-done, ...), custom_call_target="tpu_custom_call" | custom-call | tf_op jit(solution)/shard_map/apply/pallas_call | solution.py:269
Async XLA Ops:
  0.6 46.5 %copy-start = (f32[16,8192]{1,0:T(8,128)S(1)}, f32[16,8192]{1,0:T(8,128)}, u32[]{:S(2)}) copy-start(f32[16,8192]{1,0:T(8,128)} %momentum.1) | copy-start | bytes 1572868
  0.6 46.5 %copy-start.1 = (bf16[16,8192]{1,0:T(8,128)(2,1)S(1)}, bf16[16,8192]{1,0:T(8,128)(2,1)}, u32[]{:S(2)}) copy-start(bf16[16,8192]{1,0:T(8,128)(2,1)} %weight.1) | copy-start | bytes 786436
